TPU v7x, 256 devices: a whole 4x4x8 slice. The times are simulated.
256 devices in a mesh: replica: 16 (over y_hi, z), tensor: 16 (over x, y_lo, core).
Axes of the slice: x: 4, y: 4 (y_hi: 2, y_lo: 2; y = y_hi * 2 + y_lo), z: 8, core: 2. Of those that a mesh axis runs over, the one named last changes fastest.
Arguments:
- tokens_in: bfloat16 [8192, 2048], P(('replica', 'tensor')), may hold values from -6 to 6
- cotangent: bfloat16 [8192, 2048], P(('replica', 'tensor')), may hold values from -6 to 6
- gate_weight: bfloat16 [32768, 7168], P('replica', 'tensor'), may hold values from -6 to 6
- up_weight: bfloat16 [32768, 7168], P('replica', 'tensor'), may hold values from -6 to 6
- down_weight: bfloat16 [114688, 2048], P(('replica', 'tensor')), may hold values from -6 to 6
- step_index: int32 [1], replicated, may hold values from 0 to 63
Outputs:
- mixed_gate: bfloat16 [32768, 7168], P('replica', 'tensor')
- mixed_up: bfloat16 [32768, 7168], P('replica', 'tensor')
- mixed_down: bfloat16 [114688, 2048], P(('replica', 'tensor'))
- layer_out: bfloat16 [8192, 2048], P(('replica', 'tensor'))
- d_tokens: bfloat16 [8192, 2048], P(('replica', 'tensor'))
All inputs are finite; a program needn't handle non-finite values.
Results may differ from a plain program's by a relative error of at most 0.0065.
Values may be sent and summed in bfloat16 or wider, within the bound.
A program may use at most 128 MiB of HBM per device.

v0:
```python
from functools import partial

import jax
import jax.numpy as jnp
from jax import lax
from jax.sharding import PartitionSpec as P

D = 2048
FF = 7168


epsilon = 1e-05
learning_rate = 2.0


def as_sent(value):
    return jax.tree.map(lambda a: a.astype(jnp.bfloat16) if a.dtype == jnp.float32 else a, value)


def from_partner(block, axis, distance):
    count = lax.axis_size(axis)
    route = []
    for low in range(count):
        high = low | 1 << distance
        if high != low and high < count:
            route += [(low, high), (high, low)]
    return lax.ppermute(block, axis, route)


def swap_with(updated, bit_value):
    return jax.tree.map(
        lambda part, own: part.astype(own.dtype),
        from_partner(as_sent(updated), "replica", bit_value),
        updated,
    )


def gossip(updated, step_index):
    hop_count = lax.axis_size("replica").bit_length() - 1
    bit_now = step_index[0] % hop_count
    branches = [partial(swap_with, bit_value=bit_value) for bit_value in range(hop_count)]
    received = lax.switch(bit_now, branches, updated)
    return tuple(
        (
            (0.5 * (mine.astype(jnp.float32) + theirs.astype(jnp.float32))).astype(jnp.bfloat16)
            for mine, theirs in zip(updated, received)
        )
    )


def body(tokens_in, cotangent, gate_weight, up_weight, down_weight, step_index):
    scale_model = D ** (-0.5)
    scale_hidden = FF ** (-0.5)
    contract_last = (((1,), (1,)), ((), ()))
    contract_first = (((0,), (0,)), ((), ()))
    tokens_f32 = tokens_in.astype(jnp.float32)
    inverse_rms = lax.rsqrt(jnp.mean(tokens_f32 * tokens_f32, axis=-1, keepdims=True) + epsilon)
    normal_f = tokens_f32 * inverse_rms
    normed = normal_f.astype(jnp.bfloat16)
    full_normed = lax.all_gather(normed, "tensor", axis=0, tiled=True)
    gate_pre = jnp.dot(full_normed, gate_weight, preferred_element_type=jnp.float32) * scale_model
    up_pre = jnp.dot(full_normed, up_weight, preferred_element_type=jnp.float32) * scale_model
    gate_sigmoid = jax.nn.sigmoid(gate_pre)
    hidden = (gate_pre * gate_sigmoid * up_pre).astype(jnp.bfloat16)
    layer_out = lax.psum_scatter(
        jnp.dot(hidden, down_weight, preferred_element_type=jnp.float32) * scale_hidden,
        "tensor",
        scatter_dimension=0,
        tiled=True,
    ).astype(jnp.bfloat16)
    full_cotangent = lax.all_gather(cotangent, "tensor", axis=0, tiled=True)
    d_hidden = (
        lax.dot_general(
            full_cotangent, down_weight, contract_last, preferred_element_type=jnp.float32
        )
        * scale_hidden
    )
    grad_down = (
        lax.dot_general(hidden, full_cotangent, contract_first, preferred_element_type=jnp.float32)
        * scale_hidden
    )
    new_down = (down_weight.astype(jnp.float32) - learning_rate * grad_down).astype(jnp.bfloat16)
    d_gate = (d_hidden * up_pre * gate_sigmoid * (1.0 + gate_pre * (1.0 - gate_sigmoid))).astype(
        jnp.bfloat16
    )
    d_up = (d_hidden * gate_pre * gate_sigmoid).astype(jnp.bfloat16)
    grad_gate = (
        lax.dot_general(full_normed, d_gate, contract_first, preferred_element_type=jnp.float32)
        * scale_model
    )
    grad_up = (
        lax.dot_general(full_normed, d_up, contract_first, preferred_element_type=jnp.float32)
        * scale_model
    )
    new_gate = (gate_weight.astype(jnp.float32) - learning_rate * grad_gate).astype(jnp.bfloat16)
    new_up = (up_weight.astype(jnp.float32) - learning_rate * grad_up).astype(jnp.bfloat16)
    mixed_gate, mixed_up, mixed_down = gossip((new_gate, new_up, new_down), step_index)
    total = lax.dot_general(d_gate, gate_weight, contract_last, preferred_element_type=jnp.float32)
    total = total + lax.dot_general(
        d_up, up_weight, contract_last, preferred_element_type=jnp.float32
    )
    d_normed = lax.psum_scatter(total * scale_model, "tensor", scatter_dimension=0, tiled=True)
    inner = jnp.mean(d_normed * normal_f, axis=-1, keepdims=True)
    d_tokens = (inverse_rms * (d_normed - normal_f * inner)).astype(jnp.bfloat16)
    return (mixed_gate, mixed_up, mixed_down, layer_out, d_tokens)


def solution(mesh):
    in_specs = (
        P(("replica", "tensor"), None),
        P(("replica", "tensor"), None),
        P("replica", "tensor"),
        P("replica", "tensor"),
        P(("replica", "tensor"), None),
        P(),
    )
    out_specs = (
        P("replica", "tensor"),
        P("replica", "tensor"),
        P(("replica", "tensor"), None),
        P(("replica", "tensor"), None),
        P(("replica", "tensor"), None),
    )
    return jax.shard_map(body, mesh=mesh, in_specs=in_specs, out_specs=out_specs, check_vma=False)
```

profile of v0, /device:TPU:1, one launch (start us, length us, event | category | flops | bytes accessed | tf_op | source)
XLA Modules:
  0.0 338.0 jit_solution(6091016652766980232)
XLA Ops:
  7.2 0.0 all-gather.3.cloned.1.call-start
  7.2 1.0 fusion.13
  8.3 1.7 fusion.8
  9.9 0.0 all-gather.3.cloned.1.call-update
  9.9 0.0 all-gather.5.cloned.1.call-start
  10.0 0.7 all-gather.5.cloned.1.call-update
  10.7 0.0 reduce-scatter.5.cloned.1.call-start
  10.7 40.5 %all-gather.3.cloned.1.call-done = bf16[512,2048]{1,0:T(8,128)(2,1)} async-done(((bf16[32,2048]{1,0:T(8,128)(2,1)}), bf16[512,2048]{1,0:T(8,128)(2,1)}) %all-gather.3.cloned.1.call-update) | async-done | bytes 2097168 | tf_op jit(solution)/shard_map/all_gather | solution.py:60
  51.2 4.2 %convolution_multiply_fusion.1 = f32[512,448]{0,1:T(8,128)} fusion(bf16[512,2048]{1,0:T(8,128)(2,1)} %all-gather.3.cloned.1.call-done, bf16[2048,448]{0,1:T(8,128)(2,1)} %param.12), kind=kOutput, calls=%fused_computation.14 | convolution fusion | flops 939753472 | bytes 4849664 | tf_op jit(solution)/shard_map/dot_general | solution.py:61
  55.4 0.0 copy-start.1
  55.4 34.3 %all-gather.5.cloned.1.call-done = bf16[512,2048]{1,0:T(8,128)(2,1)} async-done(((bf16[32,2048]{1,0:T(8,128)(2,1)}), bf16[512,2048]{1,0:T(8,128)(2,1)}) %all-gather.5.cloned.1.call-update) | async-done | bytes 2097168 | tf_op jit(solution)/shard_map/all_gather | solution.py:71
  89.7 0.0 copy-start.7
  89.7 0.0 copy-start.9
  89.7 3.4 %convolution_multiply_fusion.3 = f32[512,448]{0,1:T(8,128)S(1)} fusion(bf16[512,2048]{1,0:T(8,128)(2,1)} %all-gather.5.cloned.1.call-done, bf16[448,2048]{1,0:T(8,128)(2,1)} %param.14), kind=kOutput, calls=%fused_computation.16 | convolution fusion | flops 939753472 | bytes 4849664 | tf_op jit(solution)/shard_map/dot_general | solution.py:73
  93.1 0.0 copy-done.1
  93.1 0.0 copy-done.7
  93.2 0.0 copy-done.9
  93.2 0.0 copy-start.2
  93.2 1.6 multiply_convert_fusion
  94.8 0.0 copy-done.2
  94.8 1.3 fusion.14
  96.1 3.4 %add_multiply_fusion = f32[512,2048]{1,0:T(8,128)} fusion(f32[512,2048]{1,0:T(8,128)S(1)} %fusion.14, bf16[512,448]{0,1:T(8,128)(2,1)S(1)} %get-tuple-element.88, bf16[2048,448]{0,1:T(8,128)(2,1)S(1)} %copy-done.1), kind=kOutput, calls=%fused_computation | convolution fusion | flops 941621248 | bytes 10682368 | tf_op jit(solution)/shard_map/dot_general | solution.py:99
  99.6 0.0 reduce-scatter.5.cloned.1.call-update
  99.6 0.0 reduce-scatter.3.cloned.1.call-start
  99.6 4.7 %convolution_multiply_fusion = f32[512,2048]{1,0:T(8,128)} fusion(bf16[512,448]{0,1:T(8,128)(2,1)S(1)} %get-tuple-element.86, bf16[448,2048]{1,0:T(8,128)(2,1)} %param.14), kind=kOutput, calls=%fused_computation.13 | convolution fusion | flops 940572672 | bytes 6488064 | tf_op jit(solution)/shard_map/dot_general | solution.py:66
  104.3 0.0 reduce-scatter.3.cloned.1.call-update
  105.0 0.0 copy-start.3
  105.0 0.0 copy-start.8
  105.1 3.4 %subtract_convert_fusion = bf16[448,2048]{1,0:T(8,128)(2,1)S(1)} fusion(bf16[448,2048]{1,0:T(8,128)(2,1)} %param.14, bf16[512,448]{0,1:T(8,128)(2,1)S(1)} %get-tuple-element.86, bf16[512,2048]{1,0:T(8,128)(2,1)} %all-gather.5.cloned.1.call-done), kind=kOutput, calls=%fused_computation.10 | convolution fusion | flops 943194112 | bytes 6225920 | tf_op jit(solution)/shard_map/dot_general | solution.py:79
  108.5 0.0 copy-done.3
  108.5 0.0 copy-done.8
  108.5 0.0 copy-start.6
  108.5 1.1 subtract_convert_fusion.2
  109.7 0.0 copy-start.4
  109.7 2.4 subtract_convert_fusion.1
  112.1 0.0 copy-done.6
  112.1 0.0 copy-done.4
  112.1 204.5 %conditional.4 = (bf16[2048,448]{0,1:T(8,128)(2,1)}, bf16[2048,448]{0,1:T(8,128)(2,1)}, bf16[448,2048]{1,0:T(8,128)(2,1)}) conditional(s32[]{:T(128)} %clamp.3, (bf16[2048,448]{0,1:T(8,128)(2,1)S(1)}, bf16[2048,448]{0,1:T(8,128)(2,1)}, bf16[448,2048]{1,0:T(8,128)(2,1)S(1)}) %tuple.58, ...), branch_computations={%region_1.0_spmd, %region_2.3_spmd, %region_3.4_spmd, %region_4.5_... | conditional | bytes 22020240
  112.1 2.4 collective-permute-start.9
  114.5 0.6 collective-permute-start.10
  115.1 2.4 collective-permute-start.11
  117.5 78.3 %collective-permute-done.9 = bf16[2048,448]{0,1:T(8,128)(2,1)} collective-permute-done((bf16[2048,448]{0,1:T(8,128)(2,1)S(1)}, bf16[2048,448]{0,1:T(8,128)(2,1)}, u32[]{:S(2)}, u32[]{:S(2)}) %collective-permute-start.9) | collective-permute-done | bytes 1835040 | tf_op jit(solution)/shard_map/cond/branch_3_fun/ppermute | solution.py:27
  195.8 59.9 %collective-permute-done.10 = bf16[2048,448]{0,1:T(8,128)(2,1)} collective-permute-done((bf16[2048,448]{0,1:T(8,128)(2,1)}, bf16[2048,448]{0,1:T(8,128)(2,1)}, u32[]{:S(2)}, u32[]{:S(2)}) %collective-permute-start.10) | collective-permute-done | bytes 1835040 | tf_op jit(solution)/shard_map/cond/branch_3_fun/ppermute | solution.py:27
  255.7 60.9 %collective-permute-done.11 = bf16[448,2048]{1,0:T(8,128)(2,1)} collective-permute-done((bf16[448,2048]{1,0:T(8,128)(2,1)S(1)}, bf16[448,2048]{1,0:T(8,128)(2,1)}, u32[]{:S(2)}, u32[]{:S(2)}) %collective-permute-start.11) | collective-permute-done | bytes 1835040 | tf_op jit(solution)/shard_map/cond/branch_3_fun/ppermute | solution.py:27
  316.6 0.0 copy-start.5
  316.6 4.2 %fusion.1 = bf16[448,2048]{1,0:T(8,128)(2,1)} fusion(bf16[448,2048]{1,0:T(8,128)(2,1)} %get-tuple-element.85, bf16[448,2048]{1,0:T(8,128)(2,1)} %copy-done.6), kind=kLoop, calls=%fused_computation.3 | loop fusion | flops 4587520 | bytes 5505024 | tf_op jit(solution)/shard_map/convert_element_type | solution.py:45
  320.7 0.0 copy-done.5
  320.7 0.0 copy-start
  320.8 6.2 %fusion.3 = (bf16[2048,448]{0,1:T(8,128)(2,1)}, bf16[2048,448]{0,1:T(8,128)(2,1)}) fusion(bf16[2048,448]{0,1:T(8,128)(2,1)} %get-tuple-element.84, bf16[2048,448]{0,1:T(8,128)(2,1)} %subtract_convert_fusion.1, bf16[2048,448]{0,1:T(8,128)(2,1)} %get-tuple-element.83, bf16[2048,448]{0,1:T(8,128)(2,1)S(1)} %copy-done.5), kind=kLoop, calls=%fused_computation.6 | loop fusion | flops 9175040 | bytes 11010048 | tf_op jit(solution)/shard_map/convert_element_type | solution.py:45
  326.9 0.0 reduce-scatter.5.cloned.1.call-done
  326.9 0.0 copy-done
  326.9 1.2 fusion.9
  328.1 1.7 fusion.12
  329.8 0.0 reduce-scatter.3.cloned.1.call-done
  329.8 1.6 convert_element_type.116
  (2 shorter events, 0.0 us)
Async XLA Ops:
  7.2 44.0 %all-gather.3.cloned.1.call-start = ((), (), s32[]{:S(2)}) async-start(), calls=%async_computation.2 | async-start | bytes 2228224 | tf_op jit(solution)/shard_map/all_gather | solution.py:60
  9.9 79.8 %all-gather.5.cloned.1.call-start = ((), (), s32[]{:S(2)}) async-start(), calls=%async_computation.3 | async-start | bytes 2228224 | tf_op jit(solution)/shard_map/all_gather | solution.py:71
  10.7 316.3 %reduce-scatter.5.cloned.1.call-start = ((), (), s32[]{:S(2)}) async-start(), calls=%async_computation.5 | async-start | bytes 4456448 | tf_op jit(solution)/shard_map/reduce_scatter | solution.py:102
  55.4 37.7 %copy-start.1 = (bf16[2048,448]{0,1:T(8,128)(2,1)S(1)}, bf16[2048,448]{0,1:T(8,128)(2,1)}, u32[]{:S(2)}) copy-start(bf16[2048,448]{0,1:T(8,128)(2,1)} %param.13) | copy-start | bytes 5505028
  89.7 3.5 %copy-start.7 = (bf16[512,2048]{1,0:T(8,128)(2,1)S(1)}, bf16[512,2048]{1,0:T(8,128)(2,1)}, u32[]{:S(2)}) copy-start(bf16[512,2048]{1,0:T(8,128)(2,1)} %all-gather.3.cloned.1.call-done) | copy-start | bytes 6291460
  89.7 3.5 %copy-start.9 = (f32[512,448]{0,1:T(8,128)S(1)}, f32[512,448]{0,1:T(8,128)}, u32[]{:S(2)}) copy-start(f32[512,448]{0,1:T(8,128)} %convolution_multiply_fusion.1) | copy-start | bytes 2752516
  93.2 1.6 copy-start.2
  99.6 230.3 %reduce-scatter.3.cloned.1.call-start = ((), (), s32[]{:S(2)}) async-start(), calls=%async_computation.4 | async-start | bytes 4456448 | tf_op jit(solution)/shard_map/reduce_scatter | solution.py:65
  105.0 3.5 %copy-start.3 = (bf16[2048,448]{0,1:T(8,128)(2,1)S(1)}, bf16[2048,448]{0,1:T(8,128)(2,1)}, u32[]{:S(2)}) copy-start(bf16[2048,448]{0,1:T(8,128)(2,1)} %param.12) | copy-start | bytes 5505028
  105.0 3.5 %copy-start.8 = (bf16[512,2048]{1,0:T(8,128)(2,1)S(1)}, bf16[512,2048]{1,0:T(8,128)(2,1)}, u32[]{:S(2)}) copy-start(bf16[512,2048]{1,0:T(8,128)(2,1)} %all-gather.3.cloned.1.call-done) | copy-start | bytes 6291460
  108.5 3.6 %copy-start.6 = (bf16[448,2048]{1,0:T(8,128)(2,1)}, bf16[448,2048]{1,0:T(8,128)(2,1)S(1)}, u32[]{:S(2)}) copy-start(bf16[448,2048]{1,0:T(8,128)(2,1)S(1)} %subtract_convert_fusion) | copy-start | bytes 5505028
  109.7 2.4 copy-start.4
  112.1 83.7 %collective-permute-start.9 = (bf16[2048,448]{0,1:T(8,128)(2,1)S(1)}, bf16[2048,448]{0,1:T(8,128)(2,1)}, u32[]{:S(2)}, u32[]{:S(2)}) collective-permute-start(bf16[2048,448]{0,1:T(8,128)(2,1)S(1)} %get-tuple-element.51), channel_id=1, source_target_pairs={{0,128},{128,0},{16,144},{144,16},{32,160},{160,32},{48,176},{176,... | collective-permute-start | bytes 5505032 | tf_op jit(solution)/shard_map/cond/branch_3_fun/ppermute | solution.py:27
  114.5 141.2 %collective-permute-start.10 = (bf16[2048,448]{0,1:T(8,128)(2,1)}, bf16[2048,448]{0,1:T(8,128)(2,1)}, u32[]{:S(2)}, u32[]{:S(2)}) collective-permute-start(bf16[2048,448]{0,1:T(8,128)(2,1)} %get-tuple-element.52), channel_id=1, source_target_pairs={{0,128},{128,0},{16,144},{144,16},{32,160},{160,32},{48,176},{176,... | collective-permute-start | bytes 5505032 | tf_op jit(solution)/shard_map/cond/branch_3_fun/ppermute | solution.py:27
  115.1 201.5 %collective-permute-start.11 = (bf16[448,2048]{1,0:T(8,128)(2,1)S(1)}, bf16[448,2048]{1,0:T(8,128)(2,1)}, u32[]{:S(2)}, u32[]{:S(2)}) collective-permute-start(bf16[448,2048]{1,0:T(8,128)(2,1)S(1)} %get-tuple-element.53), channel_id=1, source_target_pairs={{0,128},{128,0},{16,144},{144,16},{32,160},{160,32},{48,176},{176,... | collective-permute-start | bytes 5505032 | tf_op jit(solution)/shard_map/cond/branch_3_fun/ppermute | solution.py:27
  316.6 4.2 %copy-start.5 = (bf16[2048,448]{0,1:T(8,128)(2,1)S(1)}, bf16[2048,448]{0,1:T(8,128)(2,1)}, u32[]{:S(2)}) copy-start(bf16[2048,448]{0,1:T(8,128)(2,1)} %copy-done.4) | copy-start | bytes 5505028
  320.7 6.2 %copy-start = (bf16[32,2048]{1,0:T(8,128)(2,1)S(1)}, bf16[32,2048]{1,0:T(8,128)(2,1)}, u32[]{:S(2)}) copy-start(bf16[32,2048]{1,0:T(8,128)(2,1)} %param.10) | copy-start | bytes 393220
Sparse Core Ops, SparseCore 0:
  10.4 40.7 all-gather.2
  53.1 36.5 all-gather.4
  99.7 95.8 reduce-scatter.4
  198.0 101.6 reduce-scatter.2
where the time goes:
time: 338 us
  waiting for transfers between devices  275 us (81%)
  matrix products  25.7 us (8%)
  other arithmetic  17.6 us (5%)
  between operations  14.6 us (4%)
  starting transfers between devices  5.53 us (2%)
    ppermute x3, waiting for transfers between devices, from_partner(): return lax.ppermute(block, axis, route)  199 us
    all_gather x1, waiting for transfers between devices, body(): full_normed = lax.all_gather(normed, 'tensor', axis=0, tiled=True)  40.5 us
    all_gather x1, waiting for transfers between devices, body(): full_cotangent = lax.all_gather(cotangent, 'tensor', axis=0, tiled=True)  34.3 us
    convert_element_type x2, other arithmetic, gossip(): (0.5 * (mine.astype(jnp.float32) + theirs.astype(jnp.float32))).astype(jn...  10.4 us
  transfers between devices with their start and end apart: 7, of which 5 were waited for; matrix products, arithmetic and copies ran while one was open for 9% of the time, Pallas kernels for 0%

commit v1 on v0

v1 whole, which is shorter than its diff:
```python
import functools

import jax
import jax.numpy as jnp
from jax import lax
from jax.experimental import pallas as pl
from jax.experimental.pallas import tpu as pltpu
from jax.sharding import PartitionSpec as P

D = 2048
FF = 7168
EPSILON = 1e-05
RATE = 2.0
MODEL = D ** (-0.5)
HIDDEN = FF ** (-0.5)

TOK = 512
OWN = 32
PAIR = 64
ROWS = 448
STEP = 64
BLOCKS = ROWS // STEP
COLS = 256

MESH = pl.DeviceIdType.MESH
ANY = pl.BlockSpec(memory_space=pl.ANY)

RAW = (192, 128, 128, 192)


def dot(a, b, dims):
    return lax.dot_general(a, b, (dims, ((), ())), preferred_element_type=jnp.float32)


LAST = ((1,), (1,))
PLAIN = ((1,), (0,))
FIRST = ((0,), (0,))


def kernel(
    k, raw,
    tok, cot, gate, up, down,
    newo, newp, lo, dt,
    tok_v, norm_v, gath, wv, newv, praw, pnew,
    act_a, act_b, hid, d_gu, part, got, ysend, yrecv, lo_v, dt_v,
    load_sem, store_sem,
    gy_s, gy_r, gx_s, gx_r, gc_s, gc_r,
    r_s, r_r, ry_s, ry_r,
    zt_s, zt_r, zraw_s, zraw_r, znew_s, znew_r,
):
    rep, ten = lax.axis_index("replica"), lax.axis_index("tensor")
    core, y, x = lax.rem(ten, 2), lax.rem(ten // 2, 2), ten // 4
    bit = lax.rem(rep // (1 << k), 2)
    partner = (rep + (1 << k) - (2 << k) * bit, ten)
    across = (rep, ten + 2 - 4 * y)
    sibling = (rep, ten + 1 - 2 * core)

    def along_x(j):
        return (rep, lax.rem(x + j, 4) * 4 + y * 2 + core)

    def plane(j):
        q = lax.rem(core * 4 + x + j, 8)
        return (rep, lax.rem(q, 4) * 4 + y * 2 + q // 4)

    def pair_rows(c, xx):
        return pl.ds(pl.multiple_of((c * 4 + xx) * PAIR, PAIR), PAIR)

    own_rows = pl.ds(pl.multiple_of((core * 4 + x) * PAIR + y * OWN, OWN), OWN)

    def remote(src, dst, send, recv, device):
        return pltpu.make_async_remote_copy(
            src_ref=src, dst_ref=dst, send_sem=send, recv_sem=recv, device_id=device, device_id_type=MESH
        )

    load_tok = pltpu.make_async_copy(tok, tok_v, load_sem.at[0])
    load_cot = pltpu.make_async_copy(cot, gath.at[1, own_rows], load_sem.at[1])
    load_w = [
        pltpu.make_async_copy(ref, wv.at[i], load_sem.at[2 + i]) for i, ref in enumerate((gate, up, down))
    ]
    load_tok.start()
    load_cot.start()
    for c in load_w:
        c.start()

    barrier = pltpu.get_barrier_semaphore()
    for device in [partner, across] + [plane(j) for j in range(1, 8)]:
        pl.semaphore_signal(barrier, inc=1, device_id=device, device_id_type=MESH)

    load_tok.wait()
    value = tok_v[...].astype(jnp.float32)
    inverse = lax.rsqrt(jnp.mean(value * value, axis=-1, keepdims=True) + EPSILON)
    norm_v[...] = value * inverse
    gath[0, own_rows, :] = norm_v[...].astype(jnp.bfloat16)
    load_cot.wait()

    pl.semaphore_wait(barrier, 9)

    def y_copy(a):
        return remote(gath.at[a, own_rows], gath.at[a, own_rows], gy_s.at[a], gy_r.at[a], across)

    def x_copy(a, j):
        rows = pair_rows(core, x)
        return remote(gath.at[a, rows], gath.at[a, rows], gx_s.at[a, j], gx_r.at[a, j], along_x(j))

    def c_copy(a, j):
        rows = pair_rows(core, lax.rem(x + 4 - j, 4))
        return remote(gath.at[a, rows], gath.at[a, rows], gc_s.at[a, j], gc_r.at[a, j], sibling)

    def spread(a):
        y_copy(a).wait_recv()
        for j in (1, 3, 2):
            x_copy(a, j).start()
        c_copy(a, 0).start()

    def pass_on(a):
        for j in (1, 3, 2):
            x_copy(a, j).wait_recv()
            c_copy(a, j).start()

    def gathered(a):
        for j in range(4):
            c_copy(a, j).wait_recv()

    y_copy(0).start()
    y_copy(1).start()

    def z_tok(a):
        return remote(gath.at[a, own_rows], gath.at[a + 2, own_rows], zt_s.at[a], zt_r.at[a], partner)

    def z_raw(i):
        ref = (gate, up, down)[i]
        return remote(ref.at[pl.ds(0, raw)], praw.at[i], zraw_s.at[i], zraw_r.at[i], partner)

    def block(b):
        return pl.ds(pl.multiple_of(b * STEP, STEP), STEP)

    def z_new(b):
        return remote(newv.at[:, block(b)], newp.at[:, block(b)], znew_s.at[b], znew_r.at[b], partner)

    def store_own(b):
        return pltpu.make_async_copy(newv.at[:, block(b)], newo.at[:, block(b)], store_sem.at[b])

    def store_partner(b):
        return pltpu.make_async_copy(pnew.at[:, block(b)], newp.at[:, block(b)], store_sem.at[BLOCKS + b])

    z_tok(0).start()
    z_tok(1).start()
    for i in range(3):
        z_raw(i).start()

    spread(0)
    spread(1)
    pass_on(0)
    gathered(0)
    for c in load_w:
        c.wait()

    def forward(w, base, b):
        rows = block(b)
        gate_pre = dot(w[0, rows, :], gath[base], LAST) * MODEL
        up_pre = dot(w[1, rows, :], gath[base], LAST) * MODEL
        s = jax.nn.sigmoid(gate_pre)
        silu = gate_pre * s
        hid[rows, :] = (silu * up_pre).astype(jnp.bfloat16)
        act_a[rows, :] = up_pre * s * (1.0 + gate_pre * (1.0 - s))
        act_b[rows, :] = silu

    def backward(w, new, base, b):
        rows = block(b)
        d_hidden = dot(w[2, rows, :], gath[base + 1], LAST) * HIDDEN
        d_gu[0, rows, :] = (d_hidden * act_a[rows, :]).astype(jnp.bfloat16)
        d_gu[1, rows, :] = (d_hidden * act_b[rows, :]).astype(jnp.bfloat16)
        for i, (left, right, scale) in enumerate(
            ((d_gu.at[0], base, MODEL), (d_gu.at[1], base, MODEL), (hid, base + 1, HIDDEN))
        ):
            grad = dot(left[rows, :], gath[right], PLAIN) * scale
            new[i, rows, :] = (w[i, rows, :].astype(jnp.float32) - RATE * grad).astype(jnp.bfloat16)

    def loop(low, high, step):
        if high > low:
            lax.fori_loop(low, high, lambda b, _: (step(b), 0)[1], 0)

    loop(0, BLOCKS, lambda b: forward(wv, 0, b))
    pass_on(1)

    def r_copy(n, j):
        q = lax.rem(core * 4 + x + j, 8)
        rows = pl.ds(pl.multiple_of(q * PAIR, PAIR), PAIR)
        return remote(part.at[n, rows], got.at[n, j], r_s.at[n, j], r_r.at[n, j], plane(j))

    def layer(n):
        cols = pl.ds(pl.multiple_of(n * COLS, COLS), COLS)
        part[0, :, cols] = dot(hid[...], wv[2, :, cols], FIRST).astype(jnp.bfloat16)

    loop(0, D // COLS, layer)
    for j in range(1, 8):
        r_copy(0, j).start()

    gathered(1)
    for a in (0, 1):
        z_tok(a).wait_recv()
        y_copy(a + 2).start()

    first = raw // STEP

    def update_and_send(b):
        backward(wv, newv, 0, b)
        z_new(b).start()
        store_own(b).start()

    def update(b):
        backward(wv, newv, 0, b)
        store_own(b).start()

    loop(first, BLOCKS, update_and_send)
    spread(2)
    spread(3)
    loop(0, first, update)

    def back_to_input(n):
        cols = pl.ds(pl.multiple_of(n * COLS, COLS), COLS)
        total = dot(d_gu[0], wv[0, :, cols], FIRST) + dot(d_gu[1], wv[1, :, cols], FIRST)
        part[1, :, cols] = total.astype(jnp.bfloat16)

    loop(0, D // COLS, back_to_input)
    for j in range(1, 8):
        r_copy(1, j).start()
    pass_on(2)
    pass_on(3)

    mine = pl.ds(pl.multiple_of(y * OWN, OWN), OWN)
    other = pl.ds(pl.multiple_of(OWN - y * OWN, OWN), OWN)

    def ry_copy(n):
        return remote(ysend.at[n], yrecv.at[n], ry_s.at[n], ry_r.at[n], across)

    def plane_sum(n, half):
        start = pl.multiple_of((core * 4 + x) * PAIR + half * OWN, OWN)
        total = part[n, pl.ds(start, OWN), :].astype(jnp.float32)
        rows = mine if half is y else other
        for j in range(1, 8):
            total = total + got[n, j, rows, :].astype(jnp.float32)
        return total

    for n in (0, 1):
        for j in range(1, 8):
            r_copy(n, j).wait_recv()
        ysend[n] = plane_sum(n, 1 - y).astype(jnp.bfloat16)
        ry_copy(n).start()

    for a in (2, 3):
        gathered(a)
    for i in range(3):
        z_raw(i).wait_recv()

    def redo(b):
        forward(praw, 2, b)
        backward(praw, pnew, 2, b)
        store_partner(b).start()

    loop(0, first, redo)

    ry_copy(0).wait_recv()
    lo_v[...] = ((plane_sum(0, y) + yrecv[0].astype(jnp.float32)) * HIDDEN).astype(jnp.bfloat16)
    store_lo = pltpu.make_async_copy(lo_v, lo, load_sem.at[0])
    store_lo.start()
    ry_copy(1).wait_recv()
    d_normed = (plane_sum(1, y) + yrecv[1].astype(jnp.float32)) * MODEL
    inner = jnp.mean(d_normed * norm_v[...], axis=-1, keepdims=True)
    value = tok_v[...].astype(jnp.float32)
    inverse = lax.rsqrt(jnp.mean(value * value, axis=-1, keepdims=True) + EPSILON)
    dt_v[...] = (inverse * (d_normed - norm_v[...] * inner)).astype(jnp.bfloat16)
    store_dt = pltpu.make_async_copy(dt_v, dt, load_sem.at[1])
    store_dt.start()

    store_lo.wait()
    store_dt.wait()
    loop(0, BLOCKS, lambda b: store_own(b).wait())
    loop(0, first, lambda b: store_partner(b).wait())
    for a in range(4):
        y_copy(a).wait_send()
        for j in range(1, 4):
            x_copy(a, j).wait_send()
        for j in range(4):
            c_copy(a, j).wait_send()
    for n in (0, 1):
        for j in range(1, 8):
            r_copy(n, j).wait_send()
        ry_copy(n).wait_send()
        z_tok(n).wait_send()
    for i in range(3):
        z_raw(i).wait_send()
    loop(first, BLOCKS, lambda b: z_new(b).wait())


def exchange(k, tok, cot, gate, up, down):
    raw = RAW[k]
    bf, f32 = jnp.bfloat16, jnp.float32
    dma = pltpu.SemaphoreType.DMA
    stacked = jax.ShapeDtypeStruct((3, ROWS, D), bf)
    small = jax.ShapeDtypeStruct((OWN, D), bf)
    return pl.pallas_call(
        functools.partial(kernel, k, raw),
        out_shape=(stacked, stacked, small, small),
        in_specs=[ANY] * 5,
        out_specs=(ANY,) * 4,
        scratch_shapes=[
            pltpu.VMEM((OWN, D), bf),
            pltpu.VMEM((OWN, D), f32),
            pltpu.VMEM((4, TOK, D), bf),
            pltpu.VMEM((3, ROWS, D), bf),
            pltpu.VMEM((3, ROWS, D), bf),
            pltpu.VMEM((3, raw, D), bf),
            pltpu.VMEM((3, raw, D), bf),
            pltpu.VMEM((ROWS, TOK), f32),
            pltpu.VMEM((ROWS, TOK), f32),
            pltpu.VMEM((ROWS, TOK), bf),
            pltpu.VMEM((2, ROWS, TOK), bf),
            pltpu.VMEM((2, TOK, D), bf),
            pltpu.VMEM((2, 8, PAIR, D), bf),
            pltpu.VMEM((2, OWN, D), bf),
            pltpu.VMEM((2, OWN, D), bf),
            pltpu.VMEM((OWN, D), bf),
            pltpu.VMEM((OWN, D), bf),
            dma((5,)),
            dma((2 * BLOCKS,)),
            dma((4,)),
            dma((4,)),
            dma((4, 4)),
            dma((4, 4)),
            dma((4, 4)),
            dma((4, 4)),
            dma((2, 8)),
            dma((2, 8)),
            dma((2,)),
            dma((2,)),
            dma((2,)),
            dma((2,)),
            dma((3,)),
            dma((3,)),
            dma((BLOCKS,)),
            dma((BLOCKS,)),
        ],
        compiler_params=pltpu.CompilerParams(
            collective_id=k, has_side_effects=True, vmem_limit_bytes=56 * 1024 * 1024
        ),
        name=f"exchange_{k}",
    )(tok, cot, gate, up, down)


def mix_kernel(own, theirs, lo, dt, gate, up, down, lo_out, dt_out):
    for i, out in enumerate((gate, up, down)):
        total = own[i].astype(jnp.float32) + theirs[i].astype(jnp.float32)
        out[...] = (0.5 * total).astype(jnp.bfloat16)
    lo_out[...] = lo[...]
    dt_out[...] = dt[...]


def mix(own, theirs, lo, dt):
    stacked = pl.BlockSpec((3, STEP, D), lambda i: (0, i, 0))
    one = pl.BlockSpec((STEP, D), lambda i: (i, 0))
    small = pl.BlockSpec((OWN, D), lambda i: (0, 0))
    weight = jax.ShapeDtypeStruct((ROWS, D), jnp.bfloat16)
    few = jax.ShapeDtypeStruct((OWN, D), jnp.bfloat16)
    return pl.pallas_call(
        mix_kernel,
        out_shape=(weight, weight, weight, few, few),
        grid=(BLOCKS,),
        in_specs=[stacked, stacked, small, small],
        out_specs=(one, one, one, small, small),
        compiler_params=pltpu.CompilerParams(vmem_limit_bytes=24 * 1024 * 1024),
        name="mix",
    )(own, theirs, lo, dt)


def body(tokens_in, cotangent, gate_weight, up_weight, down_weight, step_index):
    k = step_index[0] % 4
    branches = [functools.partial(exchange, n) for n in range(4)]
    own, theirs, lo, dt = lax.switch(k, branches, tokens_in, cotangent, gate_weight.T, up_weight.T, down_weight)
    gate, up, down, lo, dt = mix(own, theirs, lo, dt)
    return gate.T, up.T, down, lo, dt


def solution(mesh):
    rows = P(("replica", "tensor"), None)
    split = P("replica", "tensor")
    return jax.shard_map(
        body,
        mesh=mesh,
        in_specs=(rows, rows, split, split, rows, P()),
        out_specs=(split, split, rows, rows, rows),
        check_vma=False,
    )
```

time: 338 us -> 160 us (0.47)
  waiting for transfers between devices: 275 us -> 0 us
  Pallas kernels: 0 us -> 158 us
  matrix products: 25.7 us -> 0 us
  other arithmetic: 17.6 us -> 0 us
  between operations: 14.6 us -> 1.44 us
  starting transfers between devices: 5.53 us -> 0 us
    ppermute x3 -> x0, waiting for transfers between devices: 199 us -> none  [from_partner(): return lax.ppermute(block, axis, route)]
    pallas_call x0 -> x2, Pallas kernels: none -> 158 us  [the longest x1 149 us: exchange(): pl.pallas_call(functools.partial(kernel, k, raw), out_shape=(stacked, sta...]
    all_gather x2 -> x0, waiting for transfers between devices: 74.8 us -> none  [the longest x1 40.5 us: body(): full_normed = lax.all_gather(normed, 'tensor', axis=0, tiled=True)]
    dot_general x9 -> x0, matrix products: 25.7 us -> none  [the longest x1 4.72 us: body(): jnp.dot(hidden, down_weight, preferred_element_type=jnp.float32)]
    convert_element_type x5 -> x0, other arithmetic: 15.4 us -> none  [the longest x2 10.4 us: gossip(): (0.5 * (mine.astype(jnp.float32) + theirs.astype(jnp.float32))).astype(jn...]
    ppermute x3 -> x0, starting transfers between devices: 5.37 us -> none  [from_partner(): return lax.ppermute(block, axis, route)]
  transfers between devices with their start and end apart: 7 -> 0, of which waited for: 5 -> 0; matrix products, arithmetic and copies ran while one was open for 9% -> 0% of each run, Pallas kernels for 0% -> 0%
where the time goes in v1:
time: 160 us
  Pallas kernels  158 us (99%)
    pallas_call x1, Pallas kernels, exchange(): pl.pallas_call(functools.partial(kernel, k, raw), out_shape=(stacked, sta...  149 us
    pallas_call x1, Pallas kernels, mix(): pl.pallas_call(mix_kernel, out_shape=(weight, weight, weight, few, few),...  9.08 us

profile of v1, /device:TPU:1, one launch (start us, length us, event | category | flops | bytes accessed | tf_op | source)
XLA Modules:
  0.0 160.1 jit_solution(10570228666379623048)
XLA Ops:
  1.3 149.6 %conditional.1 = ((bf16[3,448,2048]{2,1,0:T(8,128)(2,1)}, bf16[3,448,2048]{2,1,0:T(8,128)(2,1)}, bf16[32,2048]{1,0:T(8,128)(2,1)S(1)}, bf16[32,2048]{1,0:T(8,128)(2,1)S(1)})) conditional(s32[]{:T(128)} %clamp.3, (bf16[32,2048]{1,0:T(8,128)(2,1)}, bf16[32,2048]{1,0:T(8,128)(2,1)}, bf16[448,2048]{1,0:T(8,128)(2,1)}, ...), branch_computations={%region_0.1_spmd, %region_1.2_spmd, %region_2.3_spmd, %region_3.4_... | conditional | bytes 8 | solution.py:379
  1.8 148.8 %exchange_3.1 = (bf16[3,448,2048]{2,1,0:T(8,128)(2,1)}, bf16[3,448,2048]{2,1,0:T(8,128)(2,1)}, bf16[32,2048]{1,0:T(8,128)(2,1)S(1)}, bf16[32,2048]{1,0:T(8,128)(2,1)S(1)}) custom-call(bf16[32,2048]{1,0:T(8,128)(2,1)} %get-tuple-element.55.tok, bf16[32,2048]{1,0:T(8,128)(2,1)} %get-tuple-element.56.cot, bf16[448,2048]{1,0:T(8,128)(2,1)} %get-tuple-element.57.gate, ...), custom_call_target="tpu_custom_call" | custom-call | tf_op jit(solution)/shard_map/cond/branch_3_fun/exchange_3/pallas_call | solution.py:302
  150.9 9.1 %mix.1 = (bf16[448,2048]{1,0:T(8,128)(2,1)}, bf16[448,2048]{1,0:T(8,128)(2,1)}, bf16[448,2048]{1,0:T(8,128)(2,1)}, bf16[32,2048]{1,0:T(8,128)(2,1)}, bf16[32,2048]{1,0:T(8,128)(2,1)}) custom-call(bf16[3,448,2048]{2,1,0:T(8,128)(2,1)} %get-tuple-element.74.own, bf16[3,448,2048]{2,1,0:T(8,128)(2,1)} %get-tuple-element.75.theirs, ...), custom_call_target="tpu_custom_call" | custom-call | tf_op jit(solution)/shard_map/mix/pallas_call | solution.py:365
